TPU v7x, 256 devices: a whole 4x4x8 slice. The times are simulated.
256 devices in a mesh: ep: 64 (over z_lo, y, x), dp: 4 (over z_hi, core).
Axes of the slice: x: 4, y: 4, z: 8 (z_hi: 2, z_lo: 4; z = z_hi * 4 + z_lo), core: 2. Of those that a mesh axis runs over, the one named last changes fastest.
Arguments:
- tokens: bfloat16 [32768, 1792], P(('ep', 'dp')), may hold values from -6 to 6
- cotangent: bfloat16 [32768, 1792], P(('ep', 'dp')), may hold values from -6 to 6
- slot_choice: int32 [32768, 2], P(('ep', 'dp')), may hold values from 0 to 63, all different within a row; in each aligned block of 128 rows (0 to 127, 128 to 255, ...) at most 5 rows name the same one
- gate_values: float32 [32768, 2], P(('ep', 'dp')), may hold values from 0.1 to 1
- slot_expert: int32 [64], replicated, may hold values from 0 to 31, as said below
- gate_weight: bfloat16 [64, 1792, 1280], P('ep', None, 'dp'), as said below
- up_weight: bfloat16 [64, 1792, 1280], P('ep', None, 'dp'), as said below
- down_weight: bfloat16 [64, 1280, 1792], P('ep', 'dp'), as said below
Outputs:
- token_grad: bfloat16 [32768, 1792], P(('ep', 'dp'))
- down_grad: bfloat16 [64, 1280, 1792], P('ep', 'dp')
Inputs may be any that keep to these rules, and one draw needn't show every extreme that they name: `slot_choice`: each row names 2 different slots; among the rows of one device no slot is named more than 5 times, a bound that some block reaches. `slot_expert`: every expert is held by at least one slot. `gate_weight`: slots that hold the same expert have equal matrices. `up_weight`: slots that hold the same expert have equal matrices. `down_weight`: slots that hold the same expert have equal matrices.
All inputs are finite; a program needn't handle non-finite values.
Results may differ from a plain program's by a relative error of at most 0.0098.
Values may be sent and summed in bfloat16 or wider, within the bound.
No kernel may reach another device: no remote copies, remote signals or barrier semaphores. Data moves between devices by JAX's collectives and lax.ppermute only.
A program may use at most 128 MiB of HBM per device.

v0:
```python
import jax
import jax.numpy as jnp
from jax import lax
from jax.sharding import PartitionSpec as P


def in_blocks(array, dim, count):
    lengths = array.shape
    parts = array.reshape(*lengths[:dim], count, lengths[dim] // count, *lengths[dim + 1 :])
    return jnp.moveaxis(parts, dim, 0)


def cut_rows(length, count):
    unit = 8 if length >= 8 * count else 1
    return [length // unit * k // count * unit for k in range(1, count)]


def joined_along(parts, dim):
    parts = jnp.moveaxis(parts, 0, dim)
    lengths = parts.shape
    return parts.reshape(*lengths[:dim], lengths[dim] * lengths[dim + 1], *lengths[dim + 2 :])


def several_exchanges(array, axis, pieces, split_dim, concat_dim):
    parts = in_blocks(array, split_dim, lax.axis_size(axis))
    split_at = max(range(1, max(2, parts.ndim - 1)), key=lambda d: parts.shape[d])
    gathered = []
    for section in jnp.split(parts, cut_rows(parts.shape[split_at], pieces), axis=split_at):
        if section.size:
            gathered.append(lax.all_to_all(section, axis, split_axis=0, concat_axis=0, tiled=True))
    return joined_along(jnp.concatenate(gathered, axis=split_at), concat_dim)


def per_device(
    tokens, cotangent, slot_choice, gate_values, slot_expert, gate_weight, up_weight, down_weight
):
    n_slots = lax.axis_size("ep")
    tok_rows, width = tokens.shape
    topk = slot_choice.shape[1]
    capacity = max(2, 5 * tok_rows * topk // (4 * n_slots))
    rows_out = n_slots * capacity
    flat_slot = slot_choice.reshape(-1)
    onehot = (flat_slot[:, None] == jnp.arange(n_slots, dtype=jnp.int32)[None, :]).astype(jnp.int32)
    position = jnp.sum(jnp.cumsum(onehot, axis=0) * onehot, axis=1) - 1
    dest = flat_slot * capacity + position
    target = (dest[None, :] == jnp.arange(rows_out, dtype=jnp.int32)[:, None]).reshape(
        rows_out, tok_rows, topk
    )
    select = jnp.any(target, axis=2).astype(jnp.bfloat16)
    weight_table = jnp.sum(jnp.where(target, gate_values[None, :, :], 0.0), axis=2)
    sent_x = jnp.dot(select, tokens, preferred_element_type=jnp.float32).astype(jnp.bfloat16)
    sent_g = jnp.dot(
        weight_table,
        cotangent.astype(jnp.float32),
        precision=lax.Precision.HIGHEST,
        preferred_element_type=jnp.float32,
    ).astype(jnp.bfloat16)
    sent_x = sent_x.reshape(n_slots, capacity, width)
    sent_g = sent_g.reshape(n_slots, capacity, width)
    recv_x, recv_g = (
        lax.all_to_all(sent_x, "ep", split_axis=0, concat_axis=0, tiled=True),
        lax.all_to_all(sent_g, "ep", split_axis=0, concat_axis=0, tiled=True),
    )
    all_x, all_g = (
        lax.all_gather(recv_x, "dp", axis=0, tiled=True),
        lax.all_gather(recv_g, "dp", axis=0, tiled=True),
    )
    groups = all_x.shape[0] // n_slots
    rows_x = all_x.reshape(-1, width)
    rows_g = all_g.reshape(-1, width)
    w_gate = gate_weight[0]
    w_up = up_weight[0]
    w_down = down_weight[0]
    gate = jnp.dot(rows_x, w_gate, preferred_element_type=jnp.float32)
    up = jnp.dot(rows_x, w_up, preferred_element_type=jnp.float32)
    sig = jax.nn.sigmoid(gate)
    act = (gate * sig * up).astype(jnp.bfloat16)
    d_act = lax.dot_general(
        rows_g, w_down, (((1,), (1,)), ((), ())), preferred_element_type=jnp.float32
    )
    d_gate = (d_act * up * sig * (1.0 + gate * (1.0 - sig))).astype(jnp.bfloat16)
    d_up = (d_act * gate * sig).astype(jnp.bfloat16)
    partial_value = lax.dot_general(
        d_gate, w_gate, (((1,), (1,)), ((), ())), preferred_element_type=jnp.float32
    )
    partial_value = partial_value + lax.dot_general(
        d_up, w_up, (((1,), (1,)), ((), ())), preferred_element_type=jnp.float32
    )
    partial_value = partial_value.reshape(groups, n_slots, capacity, width)
    summed = lax.psum_scatter(
        partial_value.astype(jnp.bfloat16), "dp", scatter_dimension=0, tiled=True
    )
    back = lax.all_to_all(summed, "ep", split_axis=1, concat_axis=1, tiled=True)
    back = back.reshape(rows_out, width)
    token_grad = lax.dot_general(
        select, back, (((0,), (0,)), ((), ())), preferred_element_type=jnp.float32
    )
    slot_grad = lax.dot_general(
        act, rows_g, (((0,), (0,)), ((), ())), preferred_element_type=jnp.float32
    )
    hidden = slot_grad.shape[0]
    pieces = slot_grad.reshape(n_slots, -1)
    received = lax.all_to_all(
        pieces.astype(jnp.bfloat16), "ep", split_axis=0, concat_axis=0, tiled=True
    ).astype(pieces.dtype)
    same = (slot_expert[:, None] == slot_expert[None, :]).astype(jnp.float32)
    combined = jnp.dot(
        same, received, precision=lax.Precision.HIGHEST, preferred_element_type=jnp.float32
    )
    returned = several_exchanges(combined.astype(jnp.bfloat16), "ep", 2, 0, 0).astype(
        combined.dtype
    )
    down_grad = returned.reshape(1, hidden, width).astype(jnp.bfloat16)
    return (token_grad.astype(jnp.bfloat16), down_grad)


def solution(mesh):
    return jax.shard_map(
        per_device,
        mesh=mesh,
        in_specs=(
            P(("ep", "dp"), None),
            P(("ep", "dp"), None),
            P(("ep", "dp"), None),
            P(("ep", "dp"), None),
            P(),
            P("ep", None, "dp"),
            P("ep", None, "dp"),
            P("ep", "dp", None),
        ),
        out_specs=(P(("ep", "dp"), None), P("ep", "dp", None)),
        check_vma=False,
    )
```

profile of v0, /device:TPU:2, one launch (start us, length us, event | category | flops | bytes accessed | tf_op | source)
XLA Modules:
  0.0 522.7 jit_solution(6707591645249095951)
XLA Ops:
  7.2 0.9 copy.57
  8.1 0.1 eq.56
  8.2 0.1 eq.52
  8.4 0.6 reduce-window.6
  9.0 0.2 slice_reduce_fusion
  9.2 0.1 fusion.18
  9.4 0.1 sub.10
  9.5 0.1 copy.60
  9.6 0.7 multiply_add_fusion
  10.3 2.5 convolution_convert_fusion.1
  12.8 2.3 reshape.90
  15.1 56.4 %all_to_all.29 = bf16[64,5,1792]{2,1,0:T(8,128)(2,1)S(1)} all-to-all(bf16[64,5,1792]{2,1,0:T(8,128)(2,1)S(1)} %reshape.90), channel_id=1, replica_groups=mesh['ep'=64,'dp'=4] {'ep'}, dimensions={0} | all-to-all | bytes 2293760 | tf_op jit(solution)/shard_map/all_to_all | solution.py:61
  71.5 1.2 copy.63
  72.8 0.0 all-gather.3.cloned.1.call-start
  72.9 2.0 convolution_convert_fusion.2
  74.9 2.3 reshape.88
  77.2 98.8 %all_to_all.30 = bf16[64,5,1792]{2,1,0:T(8,128)(2,1)S(1)} all-to-all(bf16[64,5,1792]{2,1,0:T(8,128)(2,1)S(1)} %reshape.88), channel_id=1, replica_groups=mesh['ep'=64,'dp'=4] {'ep'}, dimensions={0} | all-to-all | bytes 2293760 | tf_op jit(solution)/shard_map/all_to_all | solution.py:62
  176.0 1.2 copy.61
  177.2 0.3 reduce-scatter.2.cloned.1.call-start
  177.6 8.1 %copy.64 = bf16[256,5,1792]{2,1,0:T(8,128)(2,1)} copy(bf16[256,5,1792]{2,0,1:T(8,128)(2,1)} %all-gather.5.cloned.1.call-done) | data formatting | bytes 9175040 | tf_op jit(solution)/shard_map/all_gather | solution.py:65
  185.6 9.8 %reshape.91 = bf16[1280,1792]{1,0:T(8,128)(2,1)} reshape(bf16[256,5,1792]{2,1,0:T(8,128)(2,1)} %copy.64) | data formatting | bytes 9175040 | tf_op jit(solution)/shard_map/reshape | solution.py:69
  195.5 4.1 fusion.6
  199.6 2.8 fusion.9
  202.5 42.7 %all-gather.3.cloned.1.call-done = bf16[256,5,1792]{2,0,1:T(8,128)(2,1)} async-done(((bf16[64,5,1792]{2,0,1:T(8,128)(2,1)}), bf16[256,5,1792]{2,0,1:T(8,128)(2,1)}) %all-gather.3.cloned.1.call-update) | async-done | bytes 4587536 | tf_op jit(solution)/shard_map/all_gather | solution.py:66
  245.2 8.1 %copy.62 = bf16[256,5,1792]{2,1,0:T(8,128)(2,1)} copy(bf16[256,5,1792]{2,0,1:T(8,128)(2,1)} %all-gather.3.cloned.1.call-done) | data formatting | bytes 9175040 | tf_op jit(solution)/shard_map/all_gather | solution.py:66
  253.3 10.0 %reshape.89 = bf16[1280,1792]{1,0:T(8,128)(2,1)} reshape(bf16[256,5,1792]{2,1,0:T(8,128)(2,1)} %copy.62) | data formatting | bytes 9175040 | tf_op jit(solution)/shard_map/reshape | solution.py:70
  263.3 4.4 fusion.11
  267.8 2.9 fusion.4
  270.7 4.9 fusion.1
  275.7 9.3 %convert_element_type.61 = bf16[4,64,5,1792]{3,2,1,0:T(8,128)(2,1)} reshape(bf16[1280,1792]{1,0:T(8,128)(2,1)} %fusion.1) | data formatting | bytes 9175040 | tf_op jit(solution)/shard_map/convert_element_type | solution.py:91
  284.9 4.7 convolution_convert_fusion.3
  289.6 0.7 convert_element_type.67
  290.3 0.5 broadcast.60
  290.8 8.6 %reduce.3 = bf16[64,8960]{1,0:T(8,128)(2,1)} reduce(bf16[64,1,8960]{2,1,0:T(2,128)(2,1)S(1)} %convert_element_type.67, bf16[]{:T(256)} %broadcast.60), dimensions={1}, to_apply=%convert_element_type.67.reduce_sub_computation | reduce | bytes 2293762 | tf_op jit(solution)/shard_map/convert_element_type | solution.py:104
  299.4 1.5 reshape.97
  300.9 117.4 %all_to_all.31 = bf16[64,2,4480]{2,1,0:T(2,128)(2,1)} all-to-all(bf16[64,2,4480]{2,1,0:T(2,128)(2,1)S(1)} %reshape.97), channel_id=1, replica_groups=mesh['ep'=64,'dp'=4] {'ep'}, dimensions={0} | all-to-all | bytes 2293760 | tf_op jit(solution)/shard_map/all_to_all | solution.py:103
  418.2 6.6 %reshape.98 = bf16[64,1,8960]{2,1,0:T(2,128)(2,1)S(1)} reshape(bf16[64,2,4480]{2,1,0:T(2,128)(2,1)} %all_to_all.31) | data formatting | bytes 2293760
  424.9 0.5 fusion
  425.4 1.5 reduce.4
  426.9 0.3 reshape.99
  427.3 35.2 %all_to_all.32 = bf16[64,2,4480]{2,1,0:T(2,128)(2,1)} all-to-all(bf16[64,2,4480]{2,1,0:T(2,128)(2,1)S(1)} %reshape.99), channel_id=1, replica_groups=mesh['ep'=64,'dp'=4] {'ep'}, dimensions={0} | all-to-all | bytes 2293760 | tf_op jit(solution)/shard_map/all_to_all | solution.py:30
  462.5 6.3 %all-to-all-start.2 = ((bf16[1,64,5,1792]{3,2,0,1:T(8,128)(2,1)}), bf16[1,64,5,1792]{3,2,0,1:T(8,128)(2,1)}, u32[]{:S(2)}, u32[]{:S(2)}) async-start(bf16[1,64,5,1792]{3,2,0,1:T(8,128)(2,1)} %bitcast.46), calls=%async_computation.3 | async-start | bytes 3670016 | tf_op jit(solution)/shard_map/all_to_all | solution.py:93
  468.8 1.0 reshape.100
  469.8 7.9 %reduce.1 = bf16[64,8960]{1,0:T(8,128)(2,1)} reduce(bf16[64,1,8960]{2,1,0:T(2,128)(2,1)S(1)} %reshape.100, bf16[]{:T(256)} %constant.25), dimensions={1}, to_apply=%all_to_all.23.reduce_sub_computation | reduce | bytes 2293762 | tf_op jit(solution)/shard_map/all_to_all | solution.py:30
  477.7 3.1 reshape.94
  480.8 31.4 %all-to-all-done.2 = bf16[1,64,5,1792]{3,2,0,1:T(8,128)(2,1)} async-done(((bf16[1,64,5,1792]{3,2,0,1:T(8,128)(2,1)}), bf16[1,64,5,1792]{3,2,0,1:T(8,128)(2,1)}, u32[]{:S(2)}, u32[]{:S(2)}) %all-to-all-start.2) | async-done | bytes 1146912 | tf_op jit(solution)/shard_map/all_to_all | solution.py:93
  512.2 2.5 reshape.92
  514.7 1.2 convolution_convert_fusion.4
  (32 shorter events, 0.3 us)
Async XLA Ops:
  7.2 188.3 %copy-start = (bf16[1,1792,320]{1,2,0:T(8,128)(2,1)S(1)}, bf16[1,1792,320]{1,2,0:T(8,128)(2,1)}, u32[]{:S(2)}) copy-start(bf16[1,1792,320]{1,2,0:T(8,128)(2,1)} %param.13) | copy-start | bytes 3440644
  7.2 170.4 %all-gather.5.cloned.1.call-start = ((), (), s32[]{:S(2)}) async-start(), calls=%async_computation.7 | async-start | bytes 5734400 | tf_op jit(solution)/shard_map/all_gather | solution.py:65
  71.5 1.3 copy-start.9
  71.5 1.4 copy-start.7
  72.8 172.5 %all-gather.3.cloned.1.call-start = ((), (), s32[]{:S(2)}) async-start(), calls=%async_computation.6 | async-start | bytes 5734400 | tf_op jit(solution)/shard_map/all_gather | solution.py:66
  177.2 285.2 %reduce-scatter.2.cloned.1.call-start = ((), (), s32[]{:S(2)}) async-start(), calls=%async_computation.8 | async-start | bytes 9175040 | tf_op jit(solution)/shard_map/reduce_scatter | solution.py:90
  195.5 4.1 copy-start.3
  195.5 4.1 copy-start.5
  263.3 4.5 copy-start.4
  267.7 3.0 copy-start.6
  418.2 6.6 %copy-start.8 = (s32[64]{0:T(128)S(1)}, s32[64]{0:T(128)}, u32[]{:S(2)}) copy-start(s32[64]{0:T(128)} %param.12) | copy-start | bytes 772
  462.5 6.3 %copy-start.2 = (bf16[64,2,4480]{2,1,0:T(2,128)(2,1)S(1)}, bf16[64,2,4480]{2,1,0:T(2,128)(2,1)}, u32[]{:S(2)}) copy-start(bf16[64,2,4480]{2,1,0:T(2,128)(2,1)} %all_to_all.32) | copy-start | bytes 3440644
  462.5 49.8 %all-to-all-start.2 = ((bf16[1,64,5,1792]{3,2,0,1:T(8,128)(2,1)}), bf16[1,64,5,1792]{3,2,0,1:T(8,128)(2,1)}, u32[]{:S(2)}, u32[]{:S(2)}) async-start(bf16[1,64,5,1792]{3,2,0,1:T(8,128)(2,1)} %bitcast.46), calls=%async_computation.3 | async-start | bytes 3670016 | tf_op jit(solution)/shard_map/all_to_all | solution.py:93
  477.7 38.2 %copy-start.1 = (bf16[1,1792,320]{1,2,0:T(8,128)(2,1)S(1)}, bf16[1,1792,320]{1,2,0:T(8,128)(2,1)}, u32[]{:S(2)}) copy-start(bf16[1,1792,320]{1,2,0:T(8,128)(2,1)} %param.13) | copy-start | bytes 3440644
Sparse Core Ops, SparseCore 0:
  72.9 92.2 all-gather.4
  177.3 67.8 all-gather.2
  285.1 125.5 reduce-scatter.1
where the time goes:
time: 528 us; the launch traced here: 523 us
  blocking collectives  308 us (58%)
  waiting for transfers between devices  74.2 us (14%)
  local copies, waits for them, and re-layouts  69.9 us (13%)
  matrix products  30.2 us (6%)
  other arithmetic  19.6 us (4%)
  between operations  14.2 us (3%)
  starting transfers between devices  6.73 us (1%)
    all_to_all x1, blocking collectives, per_device(): lax.all_to_all(pieces.astype(jnp.bfloat16), 'ep', split_axis=0, concat_ax...  117 us
    all_to_all x1, blocking collectives, per_device(): lax.all_to_all(sent_g, 'ep', split_axis=0, concat_axis=0, tiled=True)  98.8 us
    all_to_all x1, blocking collectives, per_device(): lax.all_to_all(sent_x, 'ep', split_axis=0, concat_axis=0, tiled=True)  56.4 us
    all_gather x1, waiting for transfers between devices, per_device(): lax.all_gather(recv_g, 'dp', axis=0, tiled=True)  42.7 us
    all_to_all x1, blocking collectives, several_exchanges(): lax.all_to_all(section, axis, split_axis=0, concat_axis=0, tiled=True)  35.2 us
    all_to_all x1, waiting for transfers between devices, per_device(): back = lax.all_to_all(summed, 'ep', split_axis=1, concat_axis=1, tiled=True)  31.4 us
  transfers between devices with their start and end apart: 4, of which 2 were waited for; matrix products, arithmetic and copies ran while one was open for 13% of the time, Pallas kernels for 0%

commit v1 on v0

--- a/solution.py
+++ b/solution.py
@@ -63,7 +63,9 @@
     )
     all_x, all_g = (
         lax.all_gather(recv_x, "dp", axis=0, tiled=True),
-        lax.all_gather(recv_g, "dp", axis=0, tiled=True),
+        jnp.concatenate(
+            lax.all_to_all(jnp.stack([recv_g] * lax.axis_size("dp")), "dp", 0, 0), axis=0
+        ),
     )
     groups = all_x.shape[0] // n_slots
     rows_x = all_x.reshape(-1, width)

time: 528 us -> 566 us (1.072)
  waiting for transfers between devices: 74.2 us -> 237 us
  blocking collectives: 308 us -> 156 us
  starting transfers between devices: 6.73 us -> 30.6 us
    all_to_all x0 -> x3, waiting for transfers between devices: none -> 205 us  [the longest x1 91.7 us: per_device(): lax.all_to_all(sent_g, 'ep', split_axis=0, concat_axis=0, tiled=True)]
    all_to_all x2 -> x0, blocking collectives: 155 us -> none  [the longest x1 98.8 us: per_device(): lax.all_to_all(sent_g, 'ep', split_axis=0, concat_axis=0, tiled=True)]
    all_gather x1 -> x0, waiting for transfers between devices: 42.7 us -> none  [per_device(): lax.all_gather(recv_g, 'dp', axis=0, tiled=True)]
    all_to_all x0 -> x3, starting transfers between devices: none -> 24 us  [the longest x1 12.2 us: per_device(): lax.all_to_all(sent_x, 'ep', split_axis=0, concat_axis=0, tiled=True)]
    another operation x1 -> x3, local copies, waits for them, and re-layouts: 0.01 us -> 12.6 us  [the longest x1 10 us: per_device(): rows_g = all_g.reshape(-1, width)]
    reshape x1 -> x0, local copies, waits for them, and re-layouts: 10 us -> none  [per_device(): rows_g = all_g.reshape(-1, width)]
    all_to_all x0 -> x1, local copies, waits for them, and re-layouts: none -> 8.09 us  [per_device(): lax.all_to_all(jnp.stack([recv_g] * lax.axis_size('dp')), 'dp', 0, 0)]
    all_gather x1 -> x0, local copies, waits for them, and re-layouts: 8.05 us -> none  [per_device(): lax.all_gather(recv_g, 'dp', axis=0, tiled=True)]
  transfers between devices with their start and end apart: 4 -> 6, of which waited for: 2 -> 4; matrix products, arithmetic and copies ran while one was open for 13% -> 13% of each run, Pallas kernels for 0% -> 0%
where the time goes in v1:
time: 566 us; the launch traced here: 560 us
  waiting for transfers between devices  237 us (42%)
  blocking collectives  156 us (28%)
  local copies, waits for them, and re-layouts  73.1 us (13%)
  starting transfers between devices  30.6 us (5%)
  matrix products  29.2 us (5%)
  other arithmetic  19.6 us (3%)
  between operations  14.5 us (3%)
    all_to_all x1, blocking collectives, per_device(): lax.all_to_all(pieces.astype(jnp.bfloat16), 'ep', split_axis=0, concat_ax...  120 us
    all_to_all x1, waiting for transfers between devices, per_device(): lax.all_to_all(sent_g, 'ep', split_axis=0, concat_axis=0, tiled=True)  91.7 us
    all_to_all x1, waiting for transfers between devices, per_device(): lax.all_to_all(jnp.stack([recv_g] * lax.axis_size('dp')), 'dp', 0, 0)  74.5 us
    all_to_all x1, waiting for transfers between devices, per_device(): lax.all_to_all(sent_x, 'ep', split_axis=0, concat_axis=0, tiled=True)  39.1 us
    all_to_all x1, blocking collectives, several_exchanges(): lax.all_to_all(section, axis, split_axis=0, concat_axis=0, tiled=True)  35.2 us
    all_to_all x1, waiting for transfers between devices, per_device(): back = lax.all_to_all(summed, 'ep', split_axis=1, concat_axis=1, tiled=True)  31.4 us
    all_to_all x1, starting transfers between devices, per_device(): lax.all_to_all(sent_x, 'ep', split_axis=0, concat_axis=0, tiled=True)  12.2 us
  transfers between devices with their start and end apart: 6, of which 4 were waited for; matrix products, arithmetic and copies ran while one was open for 13% of the time, Pallas kernels for 0%

profile of v1, /device:TPU:2, one launch (start us, length us, event | category | flops | bytes accessed | tf_op | source)
XLA Modules:
  0.0 559.5 jit_solution(17992024268406697842)
XLA Ops:
  7.2 0.9 copy.57
  8.2 0.1 eq.52
  8.4 0.6 reduce-window.6
  9.0 0.2 slice_reduce_fusion
  9.3 0.1 sub.10
  9.5 0.7 multiply_add_fusion
  10.3 1.5 convolution_convert_fusion.1
  11.7 1.5 reshape.88
  13.2 12.2 %all-to-all-start.2 = ((bf16[64,5,1792]{2,1,0:T(8,128)(2,1)}), bf16[64,5,1792]{2,1,0:T(8,128)(2,1)S(1)}, u32[]{:S(2)}, u32[]{:S(2)}) async-start(bf16[64,5,1792]{2,1,0:T(8,128)(2,1)} %reshape.88), calls=%async_computation.2 | async-start | bytes 3670016 | tf_op jit(solution)/shard_map/all_to_all | solution.py:61
  25.5 2.0 convolution_convert_fusion.2
  27.5 3.3 reshape.87
  30.8 39.1 %all-to-all-done.2 = bf16[64,5,1792]{2,1,0:T(8,128)(2,1)S(1)} async-done(((bf16[64,5,1792]{2,1,0:T(8,128)(2,1)}), bf16[64,5,1792]{2,1,0:T(8,128)(2,1)S(1)}, u32[]{:S(2)}, u32[]{:S(2)}) %all-to-all-start.2) | async-done | bytes 1146912 | tf_op jit(solution)/shard_map/all_to_all | solution.py:61
  70.0 6.0 %all-to-all-start = ((bf16[64,5,1792]{2,1,0:T(8,128)(2,1)}), bf16[64,5,1792]{2,1,0:T(8,128)(2,1)}, u32[]{:S(2)}, u32[]{:S(2)}) async-start(bf16[64,5,1792]{2,1,0:T(8,128)(2,1)} %reshape.87), calls=%async_computation | async-start | bytes 3670016 | tf_op jit(solution)/shard_map/all_to_all | solution.py:62
  76.1 1.2 copy.63
  77.3 91.7 %all-to-all-done = bf16[64,5,1792]{2,1,0:T(8,128)(2,1)} async-done(((bf16[64,5,1792]{2,1,0:T(8,128)(2,1)}), bf16[64,5,1792]{2,1,0:T(8,128)(2,1)}, u32[]{:S(2)}, u32[]{:S(2)}) %all-to-all-start) | async-done | bytes 1146912 | tf_op jit(solution)/shard_map/all_to_all | solution.py:62
  169.1 1.7 copy.61
  170.8 2.6 stack.2
  173.3 5.8 %all-to-all-start.1 = ((bf16[4,64,5,1792]{3,1,2,0:T(8,128)(2,1)}), bf16[4,64,5,1792]{3,1,2,0:T(8,128)(2,1)}, u32[]{:S(2)}, u32[]{:S(2)}) async-start(bf16[4,64,5,1792]{3,1,2,0:T(8,128)(2,1)} %stack.2), calls=%async_computation.1 | async-start | bytes 9175040 | tf_op jit(solution)/shard_map/all_to_all | solution.py:67
  179.1 0.3 reduce-scatter.2.cloned.1.call-start
  179.4 8.1 %copy.64 = bf16[256,5,1792]{2,1,0:T(8,128)(2,1)} copy(bf16[256,5,1792]{2,0,1:T(8,128)(2,1)} %all-gather.2.cloned.1.call-done) | data formatting | bytes 9175040 | tf_op jit(solution)/shard_map/all_gather | solution.py:65
  187.5 9.5 %reshape.89 = bf16[1280,1792]{1,0:T(8,128)(2,1)} reshape(bf16[256,5,1792]{2,1,0:T(8,128)(2,1)} %copy.64) | data formatting | bytes 9175040 | tf_op jit(solution)/shard_map/reshape | solution.py:71
  197.0 4.1 fusion.6
  201.1 2.8 fusion.9
  204.0 74.5 %all-to-all-done.1 = bf16[4,64,5,1792]{3,1,2,0:T(8,128)(2,1)} async-done(((bf16[4,64,5,1792]{3,1,2,0:T(8,128)(2,1)}), bf16[4,64,5,1792]{3,1,2,0:T(8,128)(2,1)}, u32[]{:S(2)}, u32[]{:S(2)}) %all-to-all-start.1) | async-done | bytes 4587552 | tf_op jit(solution)/shard_map/all_to_all | solution.py:67
  278.5 8.1 %copy.62 = bf16[4,64,5,1792]{3,2,1,0:T(8,128)(2,1)} copy(bf16[4,64,5,1792]{3,1,2,0:T(8,128)(2,1)} %all-to-all-done.1) | data formatting | bytes 9175040 | tf_op jit(solution)/shard_map/all_to_all | solution.py:67
  286.6 10.0 %reshape_reshape.3 = bf16[1280,1792]{1,0:T(8,128)(2,1)} reshape(bf16[4,64,5,1792]{3,2,1,0:T(8,128)(2,1)} %copy.62) | data formatting | bytes 9175040 | tf_op jit(solution)/shard_map/reshape;reshape | solution.py:72
  296.6 4.4 fusion.11
  301.1 2.9 fusion.4
  304.0 4.9 fusion.1
  309.0 9.3 %convert_element_type.61 = bf16[4,64,5,1792]{3,2,1,0:T(8,128)(2,1)} reshape(bf16[1280,1792]{1,0:T(8,128)(2,1)} %fusion.1) | data formatting | bytes 9175040 | tf_op jit(solution)/shard_map/convert_element_type | solution.py:93
  318.3 4.7 convolution_convert_fusion.3
  322.9 0.7 convert_element_type.67
  323.6 0.5 broadcast.62
  324.1 8.6 %reduce.3 = bf16[64,8960]{1,0:T(8,128)(2,1)} reduce(bf16[64,1,8960]{2,1,0:T(2,128)(2,1)S(1)} %convert_element_type.67, bf16[]{:T(256)} %broadcast.62), dimensions={1}, to_apply=%convert_element_type.67.reduce_sub_computation | reduce | bytes 2293762 | tf_op jit(solution)/shard_map/convert_element_type | solution.py:106
  332.7 1.7 reshape.95
  334.5 120.3 %all_to_all.34 = bf16[64,2,4480]{2,1,0:T(2,128)(2,1)} all-to-all(bf16[64,2,4480]{2,1,0:T(2,128)(2,1)S(1)} %reshape.95), channel_id=1, replica_groups=mesh['ep'=64,'dp'=4] {'ep'}, dimensions={0} | all-to-all | bytes 2293760 | tf_op jit(solution)/shard_map/all_to_all | solution.py:105
  454.8 6.6 %reshape.96 = bf16[64,1,8960]{2,1,0:T(2,128)(2,1)S(1)} reshape(bf16[64,2,4480]{2,1,0:T(2,128)(2,1)} %all_to_all.34) | data formatting | bytes 2293760
  461.4 0.5 fusion
  461.9 1.5 reduce.4
  463.4 0.3 reshape.97
  463.8 35.2 %all_to_all.35 = bf16[64,2,4480]{2,1,0:T(2,128)(2,1)} all-to-all(bf16[64,2,4480]{2,1,0:T(2,128)(2,1)S(1)} %reshape.97), channel_id=1, replica_groups=mesh['ep'=64,'dp'=4] {'ep'}, dimensions={0} | all-to-all | bytes 2293760 | tf_op jit(solution)/shard_map/all_to_all | solution.py:30
  499.0 6.3 %all-to-all-start.3 = ((bf16[1,64,5,1792]{3,2,0,1:T(8,128)(2,1)}), bf16[1,64,5,1792]{3,2,0,1:T(8,128)(2,1)}, u32[]{:S(2)}, u32[]{:S(2)}) async-start(bf16[1,64,5,1792]{3,2,0,1:T(8,128)(2,1)} %bitcast.46), calls=%async_computation.4 | async-start | bytes 3670016 | tf_op jit(solution)/shard_map/all_to_all | solution.py:95
  505.4 1.0 reshape.98
  506.3 7.9 %reduce.1 = bf16[64,8960]{1,0:T(8,128)(2,1)} reduce(bf16[64,1,8960]{2,1,0:T(2,128)(2,1)S(1)} %reshape.98, bf16[]{:T(256)} %constant.25), dimensions={1}, to_apply=%all_to_all.27.reduce_sub_computation | reduce | bytes 2293762 | tf_op jit(solution)/shard_map/all_to_all | solution.py:30
  514.3 3.1 reshape.92
  517.4 31.4 %all-to-all-done.3 = bf16[1,64,5,1792]{3,2,0,1:T(8,128)(2,1)} async-done(((bf16[1,64,5,1792]{3,2,0,1:T(8,128)(2,1)}), bf16[1,64,5,1792]{3,2,0,1:T(8,128)(2,1)}, u32[]{:S(2)}, u32[]{:S(2)}) %all-to-all-start.3) | async-done | bytes 1146912 | tf_op jit(solution)/shard_map/all_to_all | solution.py:95
  548.8 2.5 reshape.90
  551.2 1.2 convolution_convert_fusion.4
  (34 shorter events, 0.6 us)
Async XLA Ops:
  7.2 189.8 %copy-start = (bf16[1,1792,320]{1,2,0:T(8,128)(2,1)S(1)}, bf16[1,1792,320]{1,2,0:T(8,128)(2,1)}, u32[]{:S(2)}) copy-start(bf16[1,1792,320]{1,2,0:T(8,128)(2,1)} %param.13) | copy-start | bytes 3440644
  13.2 12.2 %copy-start.9 = (f32[128,2]{0,1:T(2,128)S(1)}, f32[128,2]{0,1:T(2,128)}, u32[]{:S(2)}) copy-start(f32[128,2]{0,1:T(2,128)} %param.11) | copy-start | bytes 3076
  13.2 12.3 %copy-start.7 = (bf16[128,1792]{1,0:T(8,128)(2,1)S(1)}, bf16[128,1792]{1,0:T(8,128)(2,1)}, u32[]{:S(2)}) copy-start(bf16[128,1792]{1,0:T(8,128)(2,1)} %param.9) | copy-start | bytes 1376260
  13.2 56.8 %all-to-all-start.2 = ((bf16[64,5,1792]{2,1,0:T(8,128)(2,1)}), bf16[64,5,1792]{2,1,0:T(8,128)(2,1)S(1)}, u32[]{:S(2)}, u32[]{:S(2)}) async-start(bf16[64,5,1792]{2,1,0:T(8,128)(2,1)} %reshape.88), calls=%async_computation.2 | async-start | bytes 3670016 | tf_op jit(solution)/shard_map/all_to_all | solution.py:61
  70.0 99.1 %all-to-all-start = ((bf16[64,5,1792]{2,1,0:T(8,128)(2,1)}), bf16[64,5,1792]{2,1,0:T(8,128)(2,1)}, u32[]{:S(2)}, u32[]{:S(2)}) async-start(bf16[64,5,1792]{2,1,0:T(8,128)(2,1)} %reshape.87), calls=%async_computation | async-start | bytes 3670016 | tf_op jit(solution)/shard_map/all_to_all | solution.py:62
  76.0 103.4 %all-gather.2.cloned.1.call-start = ((), (), s32[]{:S(2)}) async-start(), calls=%async_computation.7 | async-start | bytes 5734400 | tf_op jit(solution)/shard_map/all_gather | solution.py:65
  173.3 105.2 %all-to-all-start.1 = ((bf16[4,64,5,1792]{3,1,2,0:T(8,128)(2,1)}), bf16[4,64,5,1792]{3,1,2,0:T(8,128)(2,1)}, u32[]{:S(2)}, u32[]{:S(2)}) async-start(bf16[4,64,5,1792]{3,1,2,0:T(8,128)(2,1)} %stack.2), calls=%async_computation.1 | async-start | bytes 9175040 | tf_op jit(solution)/shard_map/all_to_all | solution.py:67
  179.1 319.9 %reduce-scatter.2.cloned.1.call-start = ((), (), s32[]{:S(2)}) async-start(), calls=%async_computation.8 | async-start | bytes 9175040 | tf_op jit(solution)/shard_map/reduce_scatter | solution.py:92
  197.0 4.1 copy-start.3
  197.0 4.1 copy-start.5
  296.6 4.5 copy-start.4
  301.1 3.0 copy-start.6
  454.8 6.6 %copy-start.8 = (s32[64]{0:T(128)S(1)}, s32[64]{0:T(128)}, u32[]{:S(2)}) copy-start(s32[64]{0:T(128)} %param.12) | copy-start | bytes 772
  499.0 6.3 %copy-start.2 = (bf16[64,2,4480]{2,1,0:T(2,128)(2,1)S(1)}, bf16[64,2,4480]{2,1,0:T(2,128)(2,1)}, u32[]{:S(2)}) copy-start(bf16[64,2,4480]{2,1,0:T(2,128)(2,1)} %all_to_all.35) | copy-start | bytes 3440644
  499.0 49.8 %all-to-all-start.3 = ((bf16[1,64,5,1792]{3,2,0,1:T(8,128)(2,1)}), bf16[1,64,5,1792]{3,2,0,1:T(8,128)(2,1)}, u32[]{:S(2)}, u32[]{:S(2)}) async-start(bf16[1,64,5,1792]{3,2,0,1:T(8,128)(2,1)} %bitcast.46), calls=%async_computation.4 | async-start | bytes 3670016 | tf_op jit(solution)/shard_map/all_to_all | solution.py:95
  514.3 38.2 %copy-start.1 = (bf16[1,1792,320]{1,2,0:T(8,128)(2,1)S(1)}, bf16[1,1792,320]{1,2,0:T(8,128)(2,1)}, u32[]{:S(2)}) copy-start(bf16[1,1792,320]{1,2,0:T(8,128)(2,1)} %param.13) | copy-start | bytes 3440644
Sparse Core Ops, SparseCore 0:
  79.3 80.7 all-gather.1
  318.4 127.5 reduce-scatter.1
